TPU v7x, 32 devices: a whole 2x2x4 slice. The times are simulated.
32 devices in a mesh: groups: 2 (over x), chan: 8 (over z, y), quad: 2 (over core).
Axes of the slice: x: 2, y: 2, z: 4, core: 2. Of those that a mesh axis runs over, the one named last changes fastest.
Arguments:
- voltages: bfloat16 [4, 256, 265216], P(('groups', 'quad'), 'chan'), parts along dimension 0, may hold values from -6 to 6
- filter_taps: float32 [4, 1024], replicated, may hold values from -0.5 to 1.5
Outputs:
- visibilities: float32 [1024, 2, 256, 512], P(('groups', 'chan'), 'quad'), parts along dimension 0
There are 2 independent parts, one for each index of `groups`. A program takes and returns all parts, laid end to end along the dimension named above; an argument that names none is the same for every part. Nothing has to cross between parts.
All inputs are finite; a program needn't handle non-finite values.
Results may differ from a plain program's by a relative error of at most 0.0047.
Values may be sent and summed in bfloat16 or wider, within the bound.
A program may use at most 320 MiB of HBM per device.

v0:
```python
import math

import jax
import jax.numpy as jnp
from jax import lax
from jax.sharding import PartitionSpec as P


def phase_table(points):
    column = jnp.arange(points, dtype=jnp.int32)
    channel = jnp.arange(points // 2, dtype=jnp.int32)
    turns = channel[:, None] * column[None, :] % points
    angles = turns.astype(jnp.float32) * jnp.float32(2.0 * math.pi / points)
    weight = jnp.float32(1.0 / math.sqrt(points))
    return jnp.concatenate([jnp.cos(angles) * weight, -jnp.sin(angles) * weight], axis=0).astype(
        jnp.bfloat16
    )


def stacked_rows(halves):
    real_part = halves[0]
    imag_part = halves[1]
    first_kind = jnp.concatenate([real_part, imag_part], axis=-1)
    second_kind = jnp.concatenate([imag_part, -imag_part * 0 - real_part], axis=-1)
    return jnp.stack([first_kind, second_kind], axis=1)


def packed_form(products, row_offset):
    row_ids = row_offset + jnp.arange(products.shape[2], dtype=jnp.int32)
    col_ids = jnp.arange(products.shape[3], dtype=jnp.int32)
    upper = col_ids[None, :] >= row_ids[:, None]
    return jnp.where(upper, products[:, 0], products[:, 1])


def on_device(voltages, filter_taps):
    tile_count = voltages.shape[1]
    taps_count = filter_taps.shape[0]
    points = filter_taps.shape[1]
    frame_count = voltages.shape[2] // points
    spectra = frame_count - taps_count + 1
    frames = voltages.reshape(tile_count, frame_count, points)
    filtered = jnp.zeros((tile_count, spectra, points), jnp.float32)
    for tap_index in range(taps_count):
        filtered = (
            filtered
            + frames[:, tap_index : tap_index + spectra, :].astype(jnp.float32)
            * filter_taps[tap_index]
        )
    filtered = filtered.astype(jnp.bfloat16)
    transform = lax.dot_general(
        phase_table(points), filtered, (((1,), (2,)), ((), ())), preferred_element_type=jnp.float32
    )
    spectra_local = transform.astype(jnp.bfloat16).reshape(2, points // 2, 1, tile_count, spectra)
    factor = jnp.float32(1.0 / spectra)
    turned = lax.all_to_all(spectra_local, "chan", split_axis=1, concat_axis=3, tiled=True)
    own_rows = turned[:, :, 0]
    left_rows = stacked_rows(own_rows)
    column_piece = lax.all_gather(turned, "quad", axis=2, tiled=True)
    merged = jnp.concatenate([column_piece[0], column_piece[1]], axis=-1)
    merged = merged.reshape(merged.shape[0], merged.shape[1] * merged.shape[2], merged.shape[3])
    products = (
        jnp.einsum("ckrs,cjs->ckrj", left_rows, merged, preferred_element_type=jnp.float32) * factor
    )
    packed = packed_form(products, lax.axis_index("quad") * own_rows.shape[2])
    return packed[:, None]


def solution(mesh):
    placed = (P(("groups", "quad"), "chan", None), P())
    return jax.shard_map(
        on_device,
        mesh=mesh,
        in_specs=placed,
        out_specs=P(("groups", "chan"), "quad", None, None),
        check_vma=False,
    )
```

profile of v0, /device:TPU:13, one launch (start us, length us, event | category | flops | bytes accessed | tf_op | source)
XLA Modules:
  0.0 656.1 jit_solution(15126735226669069623)
XLA Ops:
  6.5 0.0 all-gather.2.cloned.1.call-start
  6.5 8.6 %multiply_convert_fusion = (bf16[512,1024]{1,0:T(8,128)(2,1)S(1)}, bf16[512,1024]{1,0:T(8,128)(2,1)S(1)}) fusion(), kind=kLoop, calls=%fused_computation.32 | loop fusion | flops 9961472 | bytes 2097152 | tf_op jit(solution)/shard_map/convert.1
  15.1 0.9 fusion.30
  16.0 24.8 %reshape.24 = bf16[32,259,1024]{2,1,0:T(8,128)(2,1)} reshape(bf16[1,32,265216]{2,1,0:T(8,128)(2,1)} %param.2) | data formatting | bytes 33947648 | tf_op jit(solution)/shard_map/reshape | solution.py:41
  40.8 41.9 %fusion.17 = bf16[1024,32,256]{2,0,1:T(8,128)(2,1)} fusion(bf16[32,259,1024]{2,1,0:T(8,128)(2,1)} %reshape.24, f32[1024]{0:T(1024)S(1)} %bitcast.49, f32[1024]{0:T(1024)S(1)} %bitcast.50, f32[1024]{0:T(1024)S(1)} %bitcast.48, f32[1024]{0:T(1024)S(1)} %bitcast.47, bf16[512,1024]{1,0:T(8,128)(2,1)S(1)} %get-tuple-element.17, ...), kind=kOutput, calls=%fused_computation.21 | convolution fusion | flops 17293115392 | bytes 85999616 | tf_op jit(solution)/shard_map/dot_general | solution.py:50
  82.8 23.6 %copy.7 = bf16[2,512,1,32,256]{4,0,3,2,1:T(2,128)(2,1)S(1)} copy(bf16[2,512,1,32,256]{4,1,0,3,2:T(8,128)(2,1)} %bitcast.44) | data formatting | bytes 33554432 | tf_op jit(solution)/shard_map/reshape | solution.py:53
  106.4 365.2 %all_to_all.18 = bf16[2,512,1,32,256]{4,0,3,2,1:T(2,128)(2,1)} all-to-all(bf16[2,512,1,32,256]{4,0,3,2,1:T(2,128)(2,1)S(1)} %copy.7), channel_id=1, replica_groups=mesh['groups'=2,'chan'=8,'quad'=2] {'chan'}, dimensions={1} | all-to-all | bytes 33554432 | tf_op jit(solution)/shard_map/all_to_all | solution.py:55
  471.6 15.3 %copy.13 = bf16[2,8,64,1,32,256]{5,4,1,2,3,0:T(8,128)(2,1)} copy(bf16[2,8,64,1,32,256]{5,0,4,2,1,3:T(2,128)(2,1)} %bitcast.43) | data formatting | bytes 33554432 | tf_op jit(solution)/shard_map/all_to_all | solution.py:55
  487.0 0.0 all-gather.2.cloned.1.call-update
  487.0 0.1 iota_compare_fusion
  487.2 7.0 %fusion.29 = (bf16[1,64,1,8,32,256]{5,4,3,1,2,0:T(8,128)(2,1)S(1)}, bf16[1,64,1,8,32,256]{5,4,3,1,2,0:T(8,128)(2,1)S(1)}) fusion(bf16[2,64,1,8,32,256]{5,4,3,1,2,0:T(8,128)(2,1)} %bitcast.38), kind=kLoop, calls=%fused_computation.43 | loop fusion | bytes 33554432 | tf_op jit(solution)/shard_map/slice | solution.py:22
  494.1 0.0 copy-start
  494.1 0.0 copy-start.1
  494.2 4.5 copy-done
  498.6 5.7 copy-done.1
  504.4 6.4 multiply_subtract_fusion
  510.8 27.6 %maximum_bitcast_fusion.4 = (bf16[64,1,256,512]{3,2,1,0:T(8,128)(2,1)}, bf16[64,1,256,512]{3,2,1,0:T(8,128)(2,1)}) fusion(bf16[64,256,256]{2,1,0:T(8,128)(2,1)} %bitcast.40, bf16[64,256,256]{2,1,0:T(8,128)(2,1)} %bitcast.42, bf16[64,256,256]{2,1,0:T(8,128)(2,1)} %multiply_subtract_fusion), kind=kLoop, calls=%fused_computation.15 | loop fusion | flops 67108864 | bytes 58720256 | tf_op jit(solution)/shard_map/stack | solution.py:25
  538.4 2.9 all-gather.2.cloned.1.call-done
  541.3 23.0 %fusion.28 = (bf16[1,64,2,256,256]{4,3,2,1,0:T(8,128)(2,1)}, bf16[1,64,2,256,256]{4,3,2,1,0:T(8,128)(2,1)}) fusion(bf16[2,64,2,256,256]{4,3,2,1,0:T(8,128)(2,1)} %all-gather.2.cloned.1.call-done), kind=kLoop, calls=%fused_computation.42 | loop fusion | bytes 67108864 | tf_op jit(solution)/shard_map/slice | solution.py:59
  564.3 51.5 %broadcast_multiply_fusion = f32[64,2,256,512]{3,2,1,0:T(8,128)} fusion(bf16[64,512,256]{2,1,0:T(8,128)(2,1)} %bitcast.46, bf16[64,512,256]{2,1,0:T(8,128)(2,1)} %bitcast.45, bf16[64,1,256,512]{3,2,1,0:T(8,128)(2,1)} %get-tuple-element.12, bf16[64,1,256,512]{3,2,1,0:T(8,128)(2,1)} %get-tuple-element.11), kind=kOutput, calls=%fused_computation.8 | convolution fusion | flops 17280532480 | bytes 134217728 | tf_op jit(solution)/shard_map/ckrs,cjs->ckrj/dot_general | solution.py:62
  615.8 33.5 %slice_select_fusion = f32[64,1,256,512]{3,2,1,0:T(8,128)} fusion(f32[64,2,256,512]{3,2,1,0:T(8,128)} %broadcast_multiply_fusion, pred[256,512]{1,0:T(8,128)(4,1)S(1)} %iota_compare_fusion), kind=kLoop, calls=%fused_computation | loop fusion | flops 8388608 | bytes 100794368 | tf_op jit(solution)/shard_map/jit(_where)/select_n | solution.py:32
  (1 shorter events, 0.0 us)
Async XLA Ops:
  6.5 534.8 %all-gather.2.cloned.1.call-start = ((), (), s32[]{:S(2)}) async-start(), calls=%async_computation.1 | async-start | bytes 50331648 | tf_op jit(solution)/shard_map/all_gather | solution.py:58
  494.1 4.5 copy-start
  494.1 10.2 %copy-start.1 = (bf16[1,64,1,8,32,256]{5,4,3,1,2,0:T(8,128)(2,1)}, bf16[1,64,1,8,32,256]{5,4,3,1,2,0:T(8,128)(2,1)S(1)}, u32[]{:S(2)}) copy-start(bf16[1,64,1,8,32,256]{5,4,3,1,2,0:T(8,128)(2,1)S(1)} %get-tuple-element.8) | copy-start | bytes 25165828
Sparse Core Ops, SparseCore 0:
  487.1 54.1 all-gather.1
where the time goes:
time: 659 us; the launch traced here: 656 us
  blocking collectives  365 us (55%)
  local copies, waits for them, and re-layouts  105 us (16%)
  matrix products  93.4 us (14%)
  other arithmetic  76.2 us (12%)
  between operations  13.5 us (2%)
    all_to_all x1, blocking collectives, on_device(): lax.all_to_all(spectra_local, 'chan', split_axis=1, concat_axis=3, tiled=...  365 us
    dot_general x1, matrix products, on_device(): jnp.einsum('ckrs,cjs->ckrj', left_rows, merged, preferred_element_type=jn...  51.5 us
    dot_general x1, matrix products, on_device(): lax.dot_general(phase_table(points), filtered, (((1,), (2,)), ((), ())),...  41.9 us
    select_n x1, other arithmetic, packed_form(): return jnp.where(upper, products[:, 0], products[:, 1])  33.5 us
    another operation x1, other arithmetic, stacked_rows(): return jnp.stack([first_kind, second_kind], axis=1)  27.6 us
    reshape x1, local copies, waits for them, and re-layouts, on_device(): frames = voltages.reshape(tile_count, frame_count, points)  24.8 us
    reshape x1, local copies, waits for them, and re-layouts, on_device(): transform.astype(jnp.bfloat16)  23.6 us
    slice x1, local copies, waits for them, and re-layouts, on_device(): merged = jnp.concatenate([column_piece[0], column_piece[1]], axis=-1)  23 us
  transfers between devices with their start and end apart: 1, of which 1 were waited for; matrix products, arithmetic and copies ran while one was open for 6% of the time, Pallas kernels for 0%

commit v1 on v0

v1 whole, which is shorter than its diff:
```python
import functools
import math

import jax
import jax.numpy as jnp
import numpy as np
from jax import lax
from jax.experimental import pallas as pl
from jax.experimental.pallas import tpu as pltpu
from jax.sharding import PartitionSpec as P

MESH = pl.DeviceIdType.MESH
LANES = 128


def phase_table(points, owners):
    column = np.arange(points)
    channel = np.arange(points // 2)
    angles = ((channel[:, None] * column[None, :]) % points).astype(np.float32) * np.float32(
        2.0 * math.pi / points
    )
    weight = np.float32(1.0 / math.sqrt(points))
    table = np.stack([np.cos(angles) * weight, -np.sin(angles) * weight])
    table = table.reshape(2, owners, points // 2 // owners, points).transpose(1, 0, 2, 3)
    return table.reshape(owners, points // owners, points).astype(jnp.bfloat16)


def channelize_kernel(
    dims, volts, taps, table, out, frames, filtered, product, send, load_sem, own_sem, send_sem,
    recv_sem, pass_sem, passed_sem
):
    owners, steps, pieces, group, taps_count, points = dims
    half = owners // 2
    me = lax.axis_index("chan")
    core = lax.axis_index("quad")
    width = (LANES + taps_count - 1) * points

    def load(k):
        return pltpu.make_async_copy(
            volts.at[0, pl.ds((k // pieces) * group, group), pl.ds((k % pieces) * LANES * points, width)],
            frames.at[k % 2],
            load_sem.at[k % 2],
        )

    def partner(j):
        return ((me // half + 1 - j // half) % 2) * half + (me + j + j // half) % half

    def to_owner(k, d):
        return pltpu.make_async_remote_copy(
            src_ref=send.at[k, d],
            dst_ref=out.at[core, me, k],
            send_sem=send_sem.at[k, d],
            recv_sem=recv_sem.at[k, me],
            device_id={"chan": d},
            device_id_type=MESH,
        )

    def from_tile(k, c):
        return pltpu.make_async_remote_copy(
            src_ref=send.at[k, c],
            dst_ref=out.at[core, c, k],
            send_sem=send_sem.at[k, c],
            recv_sem=recv_sem.at[k, c],
            device_id={"chan": c},
            device_id_type=MESH,
        )

    def to_core(k, c, block):
        return pltpu.make_async_remote_copy(
            src_ref=block,
            dst_ref=out.at[core, c, k],
            send_sem=pass_sem.at[k, c],
            recv_sem=passed_sem.at[k, c],
            device_id={"quad": 1 - core},
            device_id_type=MESH,
        )

    def from_core(k, c):
        return pltpu.make_async_remote_copy(
            src_ref=send.at[k, c],
            dst_ref=out.at[1 - core, c, k],
            send_sem=pass_sem.at[k, c],
            recv_sem=passed_sem.at[k, c],
            device_id={"quad": 1 - core},
            device_id_type=MESH,
        )

    def keep(k):
        return pltpu.make_async_copy(send.at[k, me], out.at[core, me, k], own_sem.at[k])

    def filter_block(k):
        slot = k % 2

        def body(i, carry):
            rows = i // (points // LANES)
            lanes = pl.multiple_of((i % (points // LANES)) * LANES, LANES)
            gains = [taps[m : m + 1, pl.ds(lanes, LANES)] for m in range(taps_count)]
            parts = [
                frames[
                    slot, :, pl.ds(pl.multiple_of((rows * 16 + m) * points + lanes, LANES), LANES)
                ].astype(jnp.float32)
                for m in range(16 + taps_count - 1)
            ]
            sums = []
            for s in range(16):
                total = parts[s] * gains[0]
                for m in range(1, taps_count):
                    total = total + parts[s + m] * gains[m]
                sums.append(total)
            turned = jnp.swapaxes(jnp.stack(sums, axis=0), 0, 1).astype(jnp.bfloat16)
            filtered[:, pl.ds(pl.multiple_of(rows * 16, 16), 16), pl.ds(lanes, LANES)] = turned
            return carry

        lax.fori_loop(0, (LANES // 16) * (points // LANES), body, 0)

    def transform(k, d):
        def multiply(p, carry):
            pair = filtered[pl.ds(2 * p, 2)].reshape(2 * LANES, points)
            y = lax.dot_general(
                table[d], pair, (((1,), (1,)), ((), ())), preferred_element_type=jnp.float32
            )
            product[2 * p] = y[:, :LANES]
            product[2 * p + 1] = y[:, LANES:]
            return carry

        lax.fori_loop(0, group // 2, multiply, 0)

        def turn(r, carry):
            rows = pl.ds(pl.multiple_of(r * 16, 16), 16)
            send[k, d, rows] = jnp.swapaxes(product[:, rows, :], 0, 1).astype(jnp.bfloat16)
            return carry

        lax.fori_loop(0, points // owners // 16, turn, 0)

    barrier = pltpu.get_barrier_semaphore()
    load(0).start()

    def greet(j, carry):
        pl.semaphore_signal(barrier, inc=1, device_id={"chan": partner(j)}, device_id_type=MESH)
        return carry

    lax.fori_loop(0, owners - 1, greet, 0)
    pl.semaphore_signal(barrier, inc=1, device_id={"quad": 1 - core}, device_id_type=MESH)
    pl.semaphore_wait(barrier, owners)

    def step(k, carry):
        load(k).wait()

        @pl.when(k + 1 < steps)
        def _():
            load(k + 1).start()

        filter_block(k)

        def one(j, inner):
            d = partner(j)
            transform(k, d)
            to_owner(k, d).start()
            return inner

        lax.fori_loop(0, owners - 1, one, 0)
        transform(k, me)
        keep(k).start()
        to_core(k, me, send.at[k, me]).start()
        return carry

    lax.fori_loop(0, steps, step, 0)

    def forward(i, carry):
        k, c = i // (owners - 1), partner(i % (owners - 1))
        from_tile(k, c).wait_recv()
        to_core(k, c, out.at[core, c, k]).start()
        return carry

    lax.fori_loop(0, steps * (owners - 1), forward, 0)

    def finish(i, carry):
        k, c = i // (owners - 1), partner(i % (owners - 1))
        to_owner(k, c).wait_send()
        to_core(k, c, out.at[core, c, k]).wait_send()
        from_core(k, c).wait_recv()
        return carry

    lax.fori_loop(0, steps * (owners - 1), finish, 0)

    def finish_own(k, carry):
        keep(k).wait()
        to_core(k, me, send.at[k, me]).wait_send()
        from_core(k, me).wait_recv()
        return carry

    lax.fori_loop(0, steps, finish_own, 0)


def gram_kernel(channels, pieces, factor, core_ref, own, other, out):
    _, owners, groups, _, _, _, group, lanes = own.shape
    tiles = owners * groups * group
    core = core_ref[0]
    row = lax.broadcasted_iota(jnp.int32, (tiles, tiles), 0)
    col = lax.broadcasted_iota(jnp.int32, (tiles, tiles), 1)
    upper = col >= row

    def gram(a, b):
        return lax.dot_general(a, b, (((1,), (1,)), ((), ())), preferred_element_type=jnp.float32)

    def part(ref, f, kind):
        return jnp.concatenate(
            [ref[0, :, :, s, kind, f].reshape(tiles, lanes) for s in range(pieces)], axis=-1
        )

    for f in range(channels):
        re, im = part(own, f, 0), part(own, f, 1)
        other_re, other_im = part(other, f, 0), part(other, f, 1)
        right = jnp.concatenate([re, im], axis=-1)
        crossed = jnp.concatenate([im, -re], axis=-1)
        left = jnp.where(core == 0, right, crossed)
        mine = jnp.where(upper, gram(right, right), gram(crossed, right)) * factor
        cross = gram(left, jnp.concatenate([other_re, other_im], axis=-1)) * factor
        out[f, 0, :, pl.ds(pl.multiple_of(core * tiles, LANES), tiles)] = mine
        out[f, 0, :, pl.ds(pl.multiple_of((1 - core) * tiles, LANES), tiles)] = cross


def on_device(owners, voltages, filter_taps):
    tile_count = voltages.shape[1]
    taps_count, points = filter_taps.shape
    spectra = voltages.shape[2] // points - taps_count + 1
    group = min(16, tile_count)
    groups, pieces = tile_count // group, spectra // LANES
    steps = groups * pieces
    rows = points // owners
    fine = rows // 2
    exchanged = pl.pallas_call(
        functools.partial(
            channelize_kernel, (owners, steps, pieces, group, taps_count, points)
        ),
        out_shape=jax.ShapeDtypeStruct((2, owners, steps, rows, group, LANES), jnp.bfloat16),
        in_specs=[
            pl.BlockSpec(memory_space=pl.ANY),
            pl.BlockSpec(memory_space=pltpu.VMEM),
            pl.BlockSpec(memory_space=pltpu.VMEM),
        ],
        out_specs=pl.BlockSpec(memory_space=pl.ANY),
        scratch_shapes=[
            pltpu.VMEM((2, group, (LANES + taps_count - 1) * points), jnp.bfloat16),
            pltpu.VMEM((group, LANES, points), jnp.bfloat16),
            pltpu.VMEM((group, rows, LANES), jnp.float32),
            pltpu.VMEM((steps, owners, rows, group, LANES), jnp.bfloat16),
            pltpu.SemaphoreType.DMA((2,)),
            pltpu.SemaphoreType.DMA((steps,)),
            pltpu.SemaphoreType.DMA((steps, owners)),
            pltpu.SemaphoreType.DMA((steps, owners)),
            pltpu.SemaphoreType.DMA((steps, owners)),
            pltpu.SemaphoreType.DMA((steps, owners)),
        ],
        compiler_params=pltpu.CompilerParams(
            collective_id=0, has_side_effects=True, vmem_limit_bytes=52 * 2**20
        ),
    )(voltages, filter_taps, jnp.asarray(phase_table(points, owners)))
    parts = exchanged.reshape(2, owners, groups, pieces, 2, fine, group, LANES)
    block = min(4, fine)
    tiles = owners * tile_count
    core = lax.axis_index("quad").astype(jnp.int32).reshape(1)

    def spec(which):
        return pl.BlockSpec(
            (1, owners, groups, pieces, 2, block, group, LANES),
            lambda i, c: (which(c[0]), 0, 0, 0, 0, i, 0, 0),
        )

    return pl.pallas_call(
        functools.partial(gram_kernel, block, pieces, 1.0 / spectra),
        out_shape=jax.ShapeDtypeStruct((fine, 1, tiles, 2 * tiles), jnp.float32),
        grid_spec=pltpu.PrefetchScalarGridSpec(
            num_scalar_prefetch=1,
            grid=(fine // block,),
            in_specs=[spec(lambda c: c), spec(lambda c: 1 - c)],
            out_specs=pl.BlockSpec((block, 1, tiles, 2 * tiles), lambda i, c: (i, 0, 0, 0)),
        ),
        compiler_params=pltpu.CompilerParams(vmem_limit_bytes=48 * 2**20),
    )(core, parts, parts)


def solution(mesh):
    placed = (P(("groups", "quad"), "chan", None), P())
    return jax.shard_map(
        functools.partial(on_device, mesh.shape["chan"]),
        mesh=mesh,
        in_specs=placed,
        out_specs=P(("groups", "chan"), "quad", None, None),
        check_vma=False,
    )
```

time: 659 us -> 432 us (0.66)
  Pallas kernels: 0 us -> 430 us
  blocking collectives: 365 us -> 0 us
  local copies, waits for them, and re-layouts: 105 us -> 0.72 us
  matrix products: 93.4 us -> 0 us
  other arithmetic: 76.2 us -> 0 us
  between operations: 13.5 us -> 0.01 us
    pallas_call x0 -> x2, Pallas kernels: none -> 430 us  [the longest x1 396 us: on_device(): pl.pallas_call(functools.partial(channelize_kernel, (owners, steps, piece...]
    all_to_all x1 -> x0, blocking collectives: 365 us -> none  [on_device(): lax.all_to_all(spectra_local, 'chan', split_axis=1, concat_axis=3, tiled=...]
    dot_general x2 -> x0, matrix products: 93.4 us -> none  [the longest x1 51.5 us: on_device(): jnp.einsum('ckrs,cjs->ckrj', left_rows, merged, preferred_element_type=jn...]
    reshape x2 -> x0, local copies, waits for them, and re-layouts: 48.4 us -> none  [the longest x1 24.8 us: on_device(): frames = voltages.reshape(tile_count, frame_count, points)]
    another operation x2 -> x0, other arithmetic: 36.2 us -> none  [the longest x1 27.6 us: stacked_rows(): return jnp.stack([first_kind, second_kind], axis=1)]
    select_n x1 -> x0, other arithmetic: 33.5 us -> none  [packed_form(): return jnp.where(upper, products[:, 0], products[:, 1])]
    slice x3 -> x0, local copies, waits for them, and re-layouts: 30.9 us -> none  [the longest x1 23 us: on_device(): merged = jnp.concatenate([column_piece[0], column_piece[1]], axis=-1)]
    all_to_all x1 -> x0, local copies, waits for them, and re-layouts: 15.3 us -> none  [on_device(): lax.all_to_all(spectra_local, 'chan', split_axis=1, concat_axis=3, tiled=...]
  transfers between devices with their start and end apart: 1 -> 0, of which waited for: 1 -> 0; matrix products, arithmetic and copies ran while one was open for 6% -> 0% of each run, Pallas kernels for 0% -> 0%
where the time goes in v1:
time: 432 us; the launch traced here: 431 us
  Pallas kernels  430 us (100%)
    pallas_call x1, Pallas kernels, on_device(): pl.pallas_call(functools.partial(channelize_kernel, (owners, steps, piece...  396 us
    pallas_call x1, Pallas kernels, on_device(): pl.pallas_call(functools.partial(gram_kernel, block, pieces, 1.0 / spectr...  33.9 us

profile of v1, /device:TPU:13, one launch (start us, length us, event | category | flops | bytes accessed | tf_op | source)
XLA Modules:
  0.0 430.8 jit_solution(14538711265132371978)
XLA Ops:
  0.0 0.0 copy-start
  0.0 0.7 copy-done
  0.7 396.1 %shard_map.37 = bf16[2,8,4,128,16,128]{5,4,3,2,1,0:T(8,128)(2,1)} custom-call(bf16[1,32,265216]{2,1,0:T(8,128)(2,1)} %volts.1, f32[4,1024]{1,0:T(4,128)S(1)} %copy-done, bf16[8,128,1024]{2,1,0:T(8,128)(2,1)} %constant.6.clone.table), custom_call_target="tpu_custom_call" | custom-call | tf_op jit(solution)/shard_map/pallas_call | solution.py:232
  396.9 33.9 %shard_map.38 = f32[64,1,256,512]{3,2,1,0:T(8,128)} custom-call(s32[1]{0:T(128)} %bitcast.core_ref, bf16[2,8,2,2,2,64,16,128]{7,6,5,4,3,2,1,0:T(8,128)(2,1)} %bitcast.2, bf16[2,8,2,2,2,64,16,128]{7,6,5,4,3,2,1,0:T(8,128)(2,1)} %bitcast.3), custom_call_target="tpu_custom_call" | custom-call | tf_op jit(solution)/shard_map/pallas_call | solution.py:270
Async XLA Ops:
  0.0 0.7 copy-start

commit v2 on v1

--- a/solution.py
+++ b/solution.py
@@ -30,7 +30,6 @@
     recv_sem, pass_sem, passed_sem
 ):
     owners, steps, pieces, group, taps_count, points = dims
-    half = owners // 2
     me = lax.axis_index("chan")
     core = lax.axis_index("quad")
     width = (LANES + taps_count - 1) * points
@@ -43,7 +42,7 @@
         )
 
     def partner(j):
-        return ((me // half + 1 - j // half) % 2) * half + (me + j + j // half) % half
+        return (me + 1 + j) % owners
 
     def to_owner(k, d):
         return pltpu.make_async_remote_copy(
@@ -123,14 +122,14 @@
             product[2 * p + 1] = y[:, LANES:]
             return carry
 
-        lax.fori_loop(0, group // 2, multiply, 0)
+        lax.fori_loop(0, group // 2, multiply, 0, unroll=True)
 
         def turn(r, carry):
             rows = pl.ds(pl.multiple_of(r * 16, 16), 16)
             send[k, d, rows] = jnp.swapaxes(product[:, rows, :], 0, 1).astype(jnp.bfloat16)
             return carry
 
-        lax.fori_loop(0, points // owners // 16, turn, 0)
+        lax.fori_loop(0, points // owners // 16, turn, 0, unroll=True)
 
     barrier = pltpu.get_barrier_semaphore()
     load(0).start()
@@ -257,7 +256,7 @@
         ),
     )(voltages, filter_taps, jnp.asarray(phase_table(points, owners)))
     parts = exchanged.reshape(2, owners, groups, pieces, 2, fine, group, LANES)
-    block = min(4, fine)
+    block = min(16, fine)
     tiles = owners * tile_count
     core = lax.axis_index("quad").astype(jnp.int32).reshape(1)
 

time: 432 us -> 411 us (0.951)
  Pallas kernels: 430 us -> 410 us
    pallas_call x1, Pallas kernels: 396 us -> 383 us  [on_device(): pl.pallas_call(functools.partial(channelize_kernel, (owners, steps, piece...]
    pallas_call x1, Pallas kernels: 33.9 us -> 27.3 us  [on_device(): pl.pallas_call(functools.partial(gram_kernel, block, pieces, 1.0 / spectr...]
where the time goes in v2:
time: 411 us
  Pallas kernels  410 us (100%)
    pallas_call x1, Pallas kernels, on_device(): pl.pallas_call(functools.partial(channelize_kernel, (owners, steps, piece...  383 us
    pallas_call x1, Pallas kernels, on_device(): pl.pallas_call(functools.partial(gram_kernel, block, pieces, 1.0 / spectr...  27.3 us

profile of v2, /device:TPU:13, one launch (start us, length us, event | category | flops | bytes accessed | tf_op | source)
XLA Modules:
  0.0 411.0 jit_solution(1960984205508720104)
XLA Ops:
  0.0 0.0 copy-start
  0.0 0.7 copy-done
  0.7 382.9 %shard_map.37 = bf16[2,8,4,128,16,128]{5,4,3,2,1,0:T(8,128)(2,1)} custom-call(bf16[1,32,265216]{2,1,0:T(8,128)(2,1)} %volts.1, f32[4,1024]{1,0:T(4,128)S(1)} %copy-done, bf16[8,128,1024]{2,1,0:T(8,128)(2,1)} %constant.6.clone.table), custom_call_target="tpu_custom_call" | custom-call | tf_op jit(solution)/shard_map/pallas_call | solution.py:231
  383.7 27.3 %shard_map.38 = f32[64,1,256,512]{3,2,1,0:T(8,128)} custom-call(s32[1]{0:T(128)} %bitcast.core_ref, bf16[2,8,2,2,2,64,16,128]{7,6,5,4,3,2,1,0:T(8,128)(2,1)} %bitcast.2, bf16[2,8,2,2,2,64,16,128]{7,6,5,4,3,2,1,0:T(8,128)(2,1)} %bitcast.3), custom_call_target="tpu_custom_call" | custom-call | tf_op jit(solution)/shard_map/pallas_call | solution.py:269
Async XLA Ops:
  0.0 0.7 copy-start

commit v3 on v2

--- a/solution.py
+++ b/solution.py
@@ -41,8 +41,13 @@
             load_sem.at[k % 2],
         )
 
+    turn_way = 1 - 2 * core
+
     def partner(j):
-        return (me + 1 + j) % owners
+        return (me + owners + (1 + j) * turn_way) % owners
+
+    def source(j):
+        return (me + owners - (1 + j) * turn_way) % owners
 
     def to_owner(k, d):
         return pltpu.make_async_remote_copy(
@@ -166,7 +171,7 @@
     lax.fori_loop(0, steps, step, 0)
 
     def forward(i, carry):
-        k, c = i // (owners - 1), partner(i % (owners - 1))
+        k, c = i // (owners - 1), source(i % (owners - 1))
         from_tile(k, c).wait_recv()
         to_core(k, c, out.at[core, c, k]).start()
         return carry

time: 411 us -> 409 us (level)
  Pallas kernels: 410 us -> 405 us
    pallas_call x1, Pallas kernels: 383 us -> 378 us  [on_device(): pl.pallas_call(functools.partial(channelize_kernel, (owners, steps, piece...]
where the time goes in v3:
time: 409 us; the launch traced here: 406 us
  Pallas kernels  405 us (99%)
    pallas_call x1, Pallas kernels, on_device(): pl.pallas_call(functools.partial(channelize_kernel, (owners, steps, piece...  378 us
    pallas_call x1, Pallas kernels, on_device(): pl.pallas_call(functools.partial(gram_kernel, block, pieces, 1.0 / spectr...  27.3 us

profile of v3, /device:TPU:13, one launch (start us, length us, event | category | flops | bytes accessed | tf_op | source)
XLA Modules:
  0.0 406.1 jit_solution(12921153165845756593)
XLA Ops:
  0.0 0.0 copy-start
  0.0 0.7 copy-done
  0.7 378.1 %shard_map.37 = bf16[2,8,4,128,16,128]{5,4,3,2,1,0:T(8,128)(2,1)} custom-call(bf16[1,32,265216]{2,1,0:T(8,128)(2,1)} %volts.1, f32[4,1024]{1,0:T(4,128)S(1)} %copy-done, bf16[8,128,1024]{2,1,0:T(8,128)(2,1)} %constant.6.clone.table), custom_call_target="tpu_custom_call" | custom-call | tf_op jit(solution)/shard_map/pallas_call | solution.py:236
  378.8 27.3 %shard_map.38 = f32[64,1,256,512]{3,2,1,0:T(8,128)} custom-call(s32[1]{0:T(128)} %bitcast.core_ref, bf16[2,8,2,2,2,64,16,128]{7,6,5,4,3,2,1,0:T(8,128)(2,1)} %bitcast.2, bf16[2,8,2,2,2,64,16,128]{7,6,5,4,3,2,1,0:T(8,128)(2,1)} %bitcast.3), custom_call_target="tpu_custom_call" | custom-call | tf_op jit(solution)/shard_map/pallas_call | solution.py:274
Async XLA Ops:
  0.0 0.7 copy-start
